TPU v7x, 128 devices: a whole 4x4x4 slice. The times are simulated.
128 devices in a mesh: dp: 128 (over z, x, y, core).
Axes of the slice: x: 4, y: 4, z: 4, core: 2. Of those that a mesh axis runs over, the one named last changes fastest.
Arguments:
- image_embed: bfloat16 [131072, 1152], P('dp'), may hold values from -6 to 6
- text_embed: bfloat16 [131072, 1152], P('dp'), may hold values from -6 to 6
- logit_scale: float32 [1], replicated, may hold values from 4 to 16
- logit_bias: float32 [1], replicated, may hold values from -4 to -1
Outputs:
- grad_images: float32 [131072, 1152], P('dp')
- grad_texts: float32 [131072, 1152], P('dp')
All inputs are finite; a program needn't handle non-finite values.
Results may differ from a plain program's by a relative error of at most 0.005.
Values may be sent and summed in bfloat16 or wider, within the bound.
A program may use at most 128 MiB of HBM per device.

v0:
```python
import functools

import jax
import jax.numpy as jnp
from jax import lax
from jax.experimental import pallas as pl
from jax.experimental.pallas import tpu as pltpu
from jax.sharding import PartitionSpec as P

MESH = pl.DeviceIdType.MESH
CHUNKS = 4
PIECES = 16
PARTS = 8
OWN_FIRST = 2
WRITES = 4
STRIPS = 2
IMG, TXT = 0, 1
BEFORE_FAR = {2: ((0, 0),), 3: ((1, 1), (0, 2))}
AFTER_FAR = {2: ((1, 0), (0, 1)), 3: ((1, 2), (0, 3))}


def unit_rows(raw):
    values = raw.astype(jnp.float32)
    scale_row = lax.rsqrt(jnp.sum(values * values, axis=1, keepdims=True) + 1e-06)
    return values * scale_row, scale_row


def kernel(
    n,
    scale_ref,
    bias_ref,
    image_ref,
    text_ref,
    grad,
    raw,
    unit,
    far,
    cross,
    far_unit,
    terms,
    far_terms,
    cross_out,
    cross_in,
    far_out,
    far_in,
    load_sem,
    far_send,
    far_recv,
    cross_send,
    cross_recv,
    cross_out_send,
    cross_in_recv,
    far_out_send,
    far_in_recv,
):
    me = lax.axis_index("dp")
    odd = lax.rem(me, 2)
    up = lax.rem(me + n + 4 * odd - 2, n)
    down = lax.rem(me + n + 2 - 4 * odd, n)
    partner = me + 1 - 2 * odd
    still, sent = 1 - odd, odd
    rows = image_ref.shape[0]
    chunk = rows // CHUNKS
    piece = rows // PIECES
    part = rows // PARTS
    strip = rows // STRIPS

    def load(which, ref):
        return pltpu.make_async_copy(ref, raw.at[which], load_sem.at[which])

    def to_up(source, k):
        at = pl.ds(k * part, part)
        return pltpu.make_async_remote_copy(
            source.at[at], far.at[at], far_send.at[k], far_recv.at[k], device_id=(up,), device_id_type=MESH
        )

    def to_partner(source, k):
        at = pl.ds(k * part, part)
        return pltpu.make_async_remote_copy(
            source.at[at], cross.at[at], cross_send.at[k], cross_recv.at[k], device_id=(partner,), device_id_type=MESH
        )

    def terms_to_partner(j):
        at = pl.ds(j * chunk, chunk)
        return pltpu.make_async_remote_copy(
            cross_out.at[at],
            cross_in.at[at],
            cross_out_send.at[j],
            cross_in_recv.at[j],
            device_id=(partner,),
            device_id_type=MESH,
        )

    def terms_to_down(k):
        at = pl.ds(k * piece, piece)
        return pltpu.make_async_remote_copy(
            far_out.at[at], far_in.at[at], far_out_send.at[k], far_in_recv.at[k], device_id=(down,), device_id_type=MESH
        )

    load(IMG, image_ref).start()
    load(TXT, text_ref).start()
    barrier = pltpu.get_barrier_semaphore()
    for other in (up, down, partner):
        pl.semaphore_signal(barrier, inc=1, device_id=(other,), device_id_type=MESH)
    pl.semaphore_wait(barrier, 3)

    @pl.when(odd == 1)
    def _():
        for k in range(PARTS):
            to_up(text_ref, k).start()

    @pl.when(odd == 0)
    def _():
        for k in range(PARTS):
            to_up(image_ref, k).start()

    load(TXT, text_ref).wait()
    load(IMG, image_ref).wait()
    for which in (TXT, IMG):

        @pl.loop(0, PARTS)
        def _(k):
            at = pl.ds(k * part, part)
            unit[which, at] = unit_rows(raw[which, at])[0].astype(jnp.bfloat16)

        if which == TXT:

            @pl.when(odd == 0)
            def _():
                for k in range(PARTS):
                    to_partner(unit.at[TXT], k).start()

    temper = scale_ref[0]
    offset = bias_ref[0]

    def interaction(which, held, out, diagonal=None):
        y = held[...]

        def coefficients(i):
            x = unit[which, pl.ds(i * strip, strip)]
            logits = (
                temper
                * lax.dot_general(x, y, (((1,), (1,)), ((), ())), preferred_element_type=jnp.float32)
                + offset
            )
            prob = jax.nn.sigmoid(logits)
            if diagonal is not None:
                row = lax.broadcasted_iota(jnp.int32, logits.shape, 0) + i * strip
                col = lax.broadcasted_iota(jnp.int32, logits.shape, 1) + diagonal * chunk
                prob = prob - jnp.where(row == col, 1.0, 0.0)
            return x, (temper * prob).astype(jnp.bfloat16)

        ahead = coefficients(0)
        for i in range(STRIPS):
            at = pl.ds(i * strip, strip)
            x, coef = ahead
            if i < STRIPS - 1:
                ahead = coefficients(i + 1)
            mine = jnp.dot(coef, y, preferred_element_type=jnp.float32)
            theirs = lax.dot_general(coef, x, (((0,), (0,)), ((), ())), preferred_element_type=jnp.float32)
            if diagonal == 0:
                grad[which, at] = mine
            else:
                grad[which, at] += mine
            if i == 0:
                terms[...] = theirs
            elif i < STRIPS - 1:
                terms[...] += theirs
            elif diagonal is not None and diagonal >= OWN_FIRST:
                out[...] += terms[...] + theirs
            else:
                out[...] = (terms[...] + theirs).astype(out.dtype)

    per = PIECES // CHUNKS
    per_part = PARTS // CHUNKS

    def give_back(j, parity):
        @pl.when(odd == parity)
        def _():
            if parity == 1:
                terms_to_partner(j).wait_recv()
            for k in range(j * per, (j + 1) * per):
                at = pl.ds(k * piece, piece)
                total = far_terms[at]
                if parity == 1:
                    total = total + cross_in[at].astype(jnp.float32)
                far_out[at] = total.astype(jnp.bfloat16)
                terms_to_down(k).start()

    def own(j):
        at = pl.ds(j * chunk, chunk)
        interaction(IMG, unit.at[TXT, at], grad.at[TXT, at], diagonal=j)

    rest = pl.ds(OWN_FIRST * chunk, rows - OWN_FIRST * chunk)
    grad[TXT, rest] = jnp.zeros_like(grad[TXT, rest])
    for j in range(OWN_FIRST):
        own(j)

    for j in range(CHUNKS):
        at = pl.ds(j * chunk, chunk)
        for parity, earlier in BEFORE_FAR.get(j, ()):
            give_back(earlier, parity)

        @pl.loop(j * per_part, (j + 1) * per_part)
        def _(k):
            to_up(image_ref, k).wait_recv()
            here = pl.ds(k * part, part)
            far_unit[here] = unit_rows(far[here])[0].astype(jnp.bfloat16)

            @pl.when(odd == 1)
            def _():
                to_partner(far_unit, k).start()

        interaction(still, far_unit.at[at], far_terms.at[at])
        for parity, earlier in AFTER_FAR.get(j, ()):
            give_back(earlier, parity)

        @pl.loop(j * per_part, (j + 1) * per_part)
        def _(k):
            to_partner(far_unit, k).wait_recv()

        interaction(IMG, cross.at[at], cross_out.at[at])
        terms_to_partner(j).start()

    give_back(CHUNKS - 1, 1)
    for j in range(OWN_FIRST, CHUNKS):
        own(j)

    @pl.when(odd == 0)
    def _():
        @pl.loop(0, CHUNKS)
        def _(j):
            at = pl.ds(j * chunk, chunk)
            terms_to_partner(j).wait_recv()
            grad[TXT, at] += cross_in[at].astype(jnp.float32)

    def project(which, at):
        values, scale_row = unit_rows(raw[which, at])
        total = grad[which, at]
        grad[which, at] = (total - values * jnp.sum(values * total, axis=1, keepdims=True)) * scale_row

    @pl.loop(0, PIECES)
    def _(k):
        project(still, pl.ds(k * piece, piece))

    def back(k):
        at = pl.ds(k * piece, piece)
        terms_to_down(k).wait_recv()
        grad[sent, at] += far_in[at].astype(jnp.float32)
        project(sent, at)

    for j in range(CHUNKS):
        @pl.loop(j * per, (j + 1) * per)
        def _(k):
            back(k)

    for k in range(PARTS):
        to_up(image_ref, k).wait_send()
        to_partner(far_unit, k).wait_send()
    for j in range(CHUNKS):
        terms_to_partner(j).wait_send()
    for k in range(PIECES):
        terms_to_down(k).wait_send()


def write(both, image_grad, text_grad, sem):
    piece = both.shape[1] // WRITES

    def copy(which, k):
        at = pl.ds(k * piece, piece)
        return pltpu.make_async_copy(
            both.at[which, at], (image_grad, text_grad)[which].at[at], sem.at[which, k]
        )

    for k in range(WRITES):
        for which in (IMG, TXT):
            copy(which, k).start()
    for k in range(WRITES):
        for which in (IMG, TXT):
            copy(which, k).wait()


def on_device(n, image_embed, text_embed, logit_scale, logit_bias):
    rows, width = image_embed.shape
    chunk = rows // CHUNKS
    block = (rows, width)
    half = jnp.bfloat16
    dma = pltpu.SemaphoreType.DMA
    hbm = pl.BlockSpec(memory_space=pltpu.MemorySpace.HBM)
    smem = pl.BlockSpec(memory_space=pltpu.SMEM)
    grads = pl.pallas_call(
        functools.partial(kernel, n),
        out_shape=OUT((2, rows, width), jnp.float32),
        in_specs=[smem, smem, hbm, hbm],
        out_specs=pl.BlockSpec(memory_space=pltpu.VMEM),
        scratch_shapes=[
            pltpu.VMEM((2, rows, width), half),
            pltpu.VMEM((2, rows, width), half),
            pltpu.VMEM(block, half),
            pltpu.VMEM(block, half),
            pltpu.VMEM(block, half),
            pltpu.VMEM((chunk, width), jnp.float32),
            pltpu.VMEM(block, jnp.float32),
            pltpu.VMEM(block, half),
            pltpu.VMEM(block, half),
            pltpu.VMEM(block, half),
            pltpu.VMEM(block, half),
            dma((2,)),
            dma((PARTS,)),
            dma((PARTS,)),
            dma((PARTS,)),
            dma((PARTS,)),
            dma((CHUNKS,)),
            dma((CHUNKS,)),
            dma((PIECES,)),
            dma((PIECES,)),
        ],
        compiler_params=pltpu.CompilerParams(
            collective_id=0, has_side_effects=True, vmem_limit_bytes=VMEM_LIMIT
        ),
        cost_estimate=pl.CostEstimate(
            flops=18 * rows * rows * width, bytes_accessed=12 * rows * width, transcendentals=3 * rows * rows
        ),
    )(logit_scale, logit_bias, image_embed, text_embed)
    result = jax.ShapeDtypeStruct(block, jnp.float32)
    return pl.pallas_call(
        write,
        out_shape=(result, result),
        in_specs=[pl.BlockSpec(memory_space=pl.ANY)],
        out_specs=(hbm, hbm),
        compiler_params=pltpu.CompilerParams(vmem_limit_bytes=2 * 1024 * 1024),
        scratch_shapes=[dma((2, WRITES))],
        cost_estimate=pl.CostEstimate(flops=0, bytes_accessed=8 * rows * width, transcendentals=0),
    )(grads)


OUT = pltpu.MemorySpace.VMEM
VMEM_LIMIT = 50 * 1024 * 1024


def solution(mesh):
    placed = (P("dp", None), P("dp", None), P(), P())
    return jax.shard_map(
        functools.partial(on_device, mesh.shape["dp"]),
        mesh=mesh,
        in_specs=placed,
        out_specs=(P("dp", None), P("dp", None)),
        check_vma=False,
    )
```

profile of v0, /device:TPU:0, one launch (start us, length us, event | category | flops | bytes accessed | tf_op | source)
XLA Modules:
  0.0 69.0 jit_solution(5566354038690008488)
XLA Ops:
  1.9 63.3 %shard_map.59.both = f32[2,1024,1152]{2,1,0:T(8,128)S(1)} custom-call(f32[1]{0:T(128)S(6)} %copy.6.scale_ref, f32[1]{0:T(128)S(6)} %copy.7.bias_ref, bf16[1024,1152]{1,0:T(8,128)(2,1)} %image_ref.1, bf16[1024,1152]{1,0:T(8,128)(2,1)} %text_ref.1), custom_call_target="tpu_custom_call" | custom-call | flops 21743271936 | bytes 14155776 | tf_op jit(solution)/shard_map/pallas_call | solution.py:291
  65.2 3.7 %shard_map.60 = (f32[1024,1152]{1,0:T(8,128)}, f32[1024,1152]{1,0:T(8,128)}) custom-call(f32[2,1024,1152]{2,1,0:T(8,128)S(1)} %shard_map.59.both), custom_call_target="tpu_custom_call" | custom-call | bytes 9437184 | tf_op jit(solution)/shard_map/pallas_call | solution.py:326
where the time goes:
time: 69.2 us; the launch traced here: 69 us
  Pallas kernels  67 us (97%)
  between operations  2.09 us (3%)
    pallas_call x1, Pallas kernels, on_device(): pl.pallas_call(functools.partial(kernel, n), out_shape=OUT((2, rows, widt...  63.3 us
    pallas_call x1, Pallas kernels, on_device(): pl.pallas_call(write, out_shape=(result, result), in_specs=[pl.BlockSpec(...  3.7 us

commit v1 on v0

--- a/solution.py
+++ b/solution.py
@@ -15,8 +15,8 @@
 WRITES = 4
 STRIPS = 2
 IMG, TXT = 0, 1
-BEFORE_FAR = {2: ((0, 0),), 3: ((1, 1), (0, 2))}
-AFTER_FAR = {2: ((1, 0), (0, 1)), 3: ((1, 2), (0, 3))}
+BEFORE_FAR = {2: ((0, 2, 4),), 3: ((1, 4, 8), (0, 8, 12))}
+AFTER_FAR = {1: ((0, 0, 2),), 2: ((1, 0, 4), (0, 4, 8)), 3: ((1, 8, 12), (0, 12, 16))}
 
 
 def unit_rows(raw):
@@ -37,13 +37,17 @@
     far,
     cross,
     far_unit,
+    scalars,
     terms,
     far_terms,
     cross_out,
     cross_in,
     far_out,
     far_in,
+    from_down,
+    from_partner,
     load_sem,
+    scalar_sem,
     far_send,
     far_recv,
     cross_send,
@@ -68,6 +72,9 @@
     def load(which, ref):
         return pltpu.make_async_copy(ref, raw.at[which], load_sem.at[which])
 
+    def load_scalar(which, ref):
+        return pltpu.make_async_copy(ref, scalars.at[which], scalar_sem.at[which])
+
     def to_up(source, k):
         at = pl.ds(k * part, part)
         return pltpu.make_async_remote_copy(
@@ -99,10 +106,16 @@
 
     load(IMG, image_ref).start()
     load(TXT, text_ref).start()
+    load_scalar(0, scale_ref).start()
+    load_scalar(1, bias_ref).start()
     barrier = pltpu.get_barrier_semaphore()
-    for other in (up, down, partner):
-        pl.semaphore_signal(barrier, inc=1, device_id=(other,), device_id_type=MESH)
-    pl.semaphore_wait(barrier, 3)
+    pl.semaphore_signal(barrier, inc=1, device_id=(down,), device_id_type=MESH)
+
+    @pl.when(odd == 1)
+    def _():
+        pl.semaphore_signal(barrier, inc=1, device_id=(partner,), device_id_type=MESH)
+
+    pl.semaphore_wait(barrier, 2 - odd)
 
     @pl.when(odd == 1)
     def _():
@@ -113,6 +126,9 @@
     def _():
         for k in range(PARTS):
             to_up(image_ref, k).start()
+        pl.semaphore_signal(from_partner, inc=1, device_id=(partner,), device_id_type=MESH)
+
+    pl.semaphore_signal(from_down, inc=1, device_id=(up,), device_id_type=MESH)
 
     load(TXT, text_ref).wait()
     load(IMG, image_ref).wait()
@@ -130,8 +146,10 @@
                 for k in range(PARTS):
                     to_partner(unit.at[TXT], k).start()
 
-    temper = scale_ref[0]
-    offset = bias_ref[0]
+    load_scalar(0, scale_ref).wait()
+    load_scalar(1, bias_ref).wait()
+    temper = scalars[0, 0, 0]
+    offset = scalars[1, 0, 0]
 
     def interaction(which, held, out, diagonal=None):
         y = held[...]
@@ -174,12 +192,12 @@
     per = PIECES // CHUNKS
     per_part = PARTS // CHUNKS
 
-    def give_back(j, parity):
+    def give_back(parity, first, last):
         @pl.when(odd == parity)
         def _():
-            if parity == 1:
-                terms_to_partner(j).wait_recv()
-            for k in range(j * per, (j + 1) * per):
+            for k in range(first, last):
+                if parity == 1 and k % per == 0:
+                    terms_to_partner(k // per).wait_recv()
                 at = pl.ds(k * piece, piece)
                 total = far_terms[at]
                 if parity == 1:
@@ -196,10 +214,16 @@
     for j in range(OWN_FIRST):
         own(j)
 
+    pl.semaphore_wait(from_down, 1)
+
+    @pl.when(odd == 1)
+    def _():
+        pl.semaphore_wait(from_partner, 1)
+
     for j in range(CHUNKS):
         at = pl.ds(j * chunk, chunk)
-        for parity, earlier in BEFORE_FAR.get(j, ()):
-            give_back(earlier, parity)
+        for pieces in BEFORE_FAR.get(j, ()):
+            give_back(*pieces)
 
         @pl.loop(j * per_part, (j + 1) * per_part)
         def _(k):
@@ -212,8 +236,8 @@
                 to_partner(far_unit, k).start()
 
         interaction(still, far_unit.at[at], far_terms.at[at])
-        for parity, earlier in AFTER_FAR.get(j, ()):
-            give_back(earlier, parity)
+        for pieces in AFTER_FAR.get(j, ()):
+            give_back(*pieces)
 
         @pl.loop(j * per_part, (j + 1) * per_part)
         def _(k):
@@ -222,7 +246,7 @@
         interaction(IMG, cross.at[at], cross_out.at[at])
         terms_to_partner(j).start()
 
-    give_back(CHUNKS - 1, 1)
+    give_back(1, PIECES - per, PIECES)
     for j in range(OWN_FIRST, CHUNKS):
         own(j)
 
@@ -287,11 +311,10 @@
     half = jnp.bfloat16
     dma = pltpu.SemaphoreType.DMA
     hbm = pl.BlockSpec(memory_space=pltpu.MemorySpace.HBM)
-    smem = pl.BlockSpec(memory_space=pltpu.SMEM)
     grads = pl.pallas_call(
         functools.partial(kernel, n),
         out_shape=OUT((2, rows, width), jnp.float32),
-        in_specs=[smem, smem, hbm, hbm],
+        in_specs=[hbm] * 4,
         out_specs=pl.BlockSpec(memory_space=pltpu.VMEM),
         scratch_shapes=[
             pltpu.VMEM((2, rows, width), half),
@@ -299,12 +322,16 @@
             pltpu.VMEM(block, half),
             pltpu.VMEM(block, half),
             pltpu.VMEM(block, half),
+            pltpu.SMEM((2, 1, 1), jnp.float32),
             pltpu.VMEM((chunk, width), jnp.float32),
             pltpu.VMEM(block, jnp.float32),
             pltpu.VMEM(block, half),
             pltpu.VMEM(block, half),
             pltpu.VMEM(block, half),
             pltpu.VMEM(block, half),
+            pltpu.SemaphoreType.REGULAR,
+            pltpu.SemaphoreType.REGULAR,
+            dma((2,)),
             dma((2,)),
             dma((PARTS,)),
             dma((PARTS,)),
@@ -321,7 +348,7 @@
         cost_estimate=pl.CostEstimate(
             flops=18 * rows * rows * width, bytes_accessed=12 * rows * width, transcendentals=3 * rows * rows
         ),
-    )(logit_scale, logit_bias, image_embed, text_embed)
+    )(logit_scale.reshape(1, 1), logit_bias.reshape(1, 1), image_embed, text_embed)
     result = jax.ShapeDtypeStruct(block, jnp.float32)
     return pl.pallas_call(
         write,

time: 69.2 us -> 68.4 us (0.988); the launches traced: 69 us -> 67.1 us
  Pallas kernels: 67 us -> 65 us
    pallas_call x1, Pallas kernels: 63.3 us -> 61.3 us  [on_device(): pl.pallas_call(functools.partial(kernel, n), out_shape=OUT((2, rows, widt...]
where the time goes in v1:
time: 68.4 us; the launch traced here: 67.1 us
  Pallas kernels  65 us (95%)
  between operations  2.09 us (3%)
    pallas_call x1, Pallas kernels, on_device(): pl.pallas_call(functools.partial(kernel, n), out_shape=OUT((2, rows, widt...  61.3 us
    pallas_call x1, Pallas kernels, on_device(): pl.pallas_call(write, out_shape=(result, result), in_specs=[pl.BlockSpec(...  3.7 us

profile of v1, /device:TPU:0, one launch (start us, length us, event | category | flops | bytes accessed | tf_op | source)
XLA Modules:
  0.0 67.1 jit_solution(3688914789573815116)
XLA Ops:
  1.9 61.3 %shard_map.59.both = f32[2,1024,1152]{2,1,0:T(8,128)S(1)} custom-call(f32[1,1]{1,0:T(1,128)} %bitcast.2.scale_ref, f32[1,1]{1,0:T(1,128)} %bitcast.3.bias_ref, bf16[1024,1152]{1,0:T(8,128)(2,1)} %image_ref.1, bf16[1024,1152]{1,0:T(8,128)(2,1)} %text_ref.1), custom_call_target="tpu_custom_call" | custom-call | flops 21743271936 | bytes 14155776 | tf_op jit(solution)/shard_map/pallas_call | solution.py:314
  63.2 3.7 %shard_map.60 = (f32[1024,1152]{1,0:T(8,128)}, f32[1024,1152]{1,0:T(8,128)}) custom-call(f32[2,1024,1152]{2,1,0:T(8,128)S(1)} %shard_map.59.both), custom_call_target="tpu_custom_call" | custom-call | bytes 9437184 | tf_op jit(solution)/shard_map/pallas_call | solution.py:353

commit v2 on v1

--- a/solution.py
+++ b/solution.py
@@ -37,7 +37,6 @@
     far,
     cross,
     far_unit,
-    scalars,
     terms,
     far_terms,
     cross_out,
@@ -47,7 +46,6 @@
     from_down,
     from_partner,
     load_sem,
-    scalar_sem,
     far_send,
     far_recv,
     cross_send,
@@ -72,9 +70,6 @@
     def load(which, ref):
         return pltpu.make_async_copy(ref, raw.at[which], load_sem.at[which])
 
-    def load_scalar(which, ref):
-        return pltpu.make_async_copy(ref, scalars.at[which], scalar_sem.at[which])
-
     def to_up(source, k):
         at = pl.ds(k * part, part)
         return pltpu.make_async_remote_copy(
@@ -104,10 +99,6 @@
             far_out.at[at], far_in.at[at], far_out_send.at[k], far_in_recv.at[k], device_id=(down,), device_id_type=MESH
         )
 
-    load(IMG, image_ref).start()
-    load(TXT, text_ref).start()
-    load_scalar(0, scale_ref).start()
-    load_scalar(1, bias_ref).start()
     barrier = pltpu.get_barrier_semaphore()
     pl.semaphore_signal(barrier, inc=1, device_id=(down,), device_id_type=MESH)
 
@@ -129,6 +120,9 @@
         pl.semaphore_signal(from_partner, inc=1, device_id=(partner,), device_id_type=MESH)
 
     pl.semaphore_signal(from_down, inc=1, device_id=(up,), device_id_type=MESH)
+
+    load(IMG, image_ref).start()
+    load(TXT, text_ref).start()
 
     load(TXT, text_ref).wait()
     load(IMG, image_ref).wait()
@@ -146,10 +140,8 @@
                 for k in range(PARTS):
                     to_partner(unit.at[TXT], k).start()
 
-    load_scalar(0, scale_ref).wait()
-    load_scalar(1, bias_ref).wait()
-    temper = scalars[0, 0, 0]
-    offset = scalars[1, 0, 0]
+    temper = scale_ref[0]
+    offset = bias_ref[0]
 
     def interaction(which, held, out, diagonal=None):
         y = held[...]
@@ -267,23 +259,18 @@
     def _(k):
         project(still, pl.ds(k * piece, piece))
 
-    def back(k):
-        at = pl.ds(k * piece, piece)
-        terms_to_down(k).wait_recv()
-        grad[sent, at] += far_in[at].astype(jnp.float32)
-        project(sent, at)
-
-    for j in range(CHUNKS):
-        @pl.loop(j * per, (j + 1) * per)
-        def _(k):
-            back(k)
-
     for k in range(PARTS):
         to_up(image_ref, k).wait_send()
         to_partner(far_unit, k).wait_send()
     for j in range(CHUNKS):
         terms_to_partner(j).wait_send()
-    for k in range(PIECES):
+
+    @pl.loop(0, PIECES)
+    def _(k):
+        at = pl.ds(k * piece, piece)
+        terms_to_down(k).wait_recv()
+        grad[sent, at] += far_in[at].astype(jnp.float32)
+        project(sent, at)
         terms_to_down(k).wait_send()
 
 
@@ -311,10 +298,11 @@
     half = jnp.bfloat16
     dma = pltpu.SemaphoreType.DMA
     hbm = pl.BlockSpec(memory_space=pltpu.MemorySpace.HBM)
+    smem = pl.BlockSpec(memory_space=pltpu.SMEM)
     grads = pl.pallas_call(
         functools.partial(kernel, n),
         out_shape=OUT((2, rows, width), jnp.float32),
-        in_specs=[hbm] * 4,
+        in_specs=[smem, smem, hbm, hbm],
         out_specs=pl.BlockSpec(memory_space=pltpu.VMEM),
         scratch_shapes=[
             pltpu.VMEM((2, rows, width), half),
@@ -322,7 +310,6 @@
             pltpu.VMEM(block, half),
             pltpu.VMEM(block, half),
             pltpu.VMEM(block, half),
-            pltpu.SMEM((2, 1, 1), jnp.float32),
             pltpu.VMEM((chunk, width), jnp.float32),
             pltpu.VMEM(block, jnp.float32),
             pltpu.VMEM(block, half),
@@ -331,7 +318,6 @@
             pltpu.VMEM(block, half),
             pltpu.SemaphoreType.REGULAR,
             pltpu.SemaphoreType.REGULAR,
-            dma((2,)),
             dma((2,)),
             dma((PARTS,)),
             dma((PARTS,)),
@@ -348,7 +334,7 @@
         cost_estimate=pl.CostEstimate(
             flops=18 * rows * rows * width, bytes_accessed=12 * rows * width, transcendentals=3 * rows * rows
         ),
-    )(logit_scale.reshape(1, 1), logit_bias.reshape(1, 1), image_embed, text_embed)
+    )(logit_scale, logit_bias, image_embed, text_embed)
     result = jax.ShapeDtypeStruct(block, jnp.float32)
     return pl.pallas_call(
         write,

time: 68.4 us -> 68.3 us (level)
  no operation moved by 1% of the time
where the time goes in v2:
time: 68.3 us; the launch traced here: 67 us
  Pallas kernels  64.9 us (95%)
  between operations  2.09 us (3%)
    pallas_call x1, Pallas kernels, on_device(): pl.pallas_call(functools.partial(kernel, n), out_shape=OUT((2, rows, widt...  61.2 us
    pallas_call x1, Pallas kernels, on_device(): pl.pallas_call(write, out_shape=(result, result), in_specs=[pl.BlockSpec(...  3.7 us

profile of v2, /device:TPU:0, one launch (start us, length us, event | category | flops | bytes accessed | tf_op | source)
XLA Modules:
  0.0 67.0 jit_solution(9202671525926628640)
XLA Ops:
  1.9 61.2 %shard_map.59.both = f32[2,1024,1152]{2,1,0:T(8,128)S(1)} custom-call(f32[1]{0:T(128)S(6)} %copy.6.scale_ref, f32[1]{0:T(128)S(6)} %copy.7.bias_ref, bf16[1024,1152]{1,0:T(8,128)(2,1)} %image_ref.1, bf16[1024,1152]{1,0:T(8,128)(2,1)} %text_ref.1), custom_call_target="tpu_custom_call" | custom-call | flops 21743271936 | bytes 14155776 | tf_op jit(solution)/shard_map/pallas_call | solution.py:302
  63.1 3.7 %shard_map.60 = (f32[1024,1152]{1,0:T(8,128)}, f32[1024,1152]{1,0:T(8,128)}) custom-call(f32[2,1024,1152]{2,1,0:T(8,128)S(1)} %shard_map.59.both), custom_call_target="tpu_custom_call" | custom-call | bytes 9437184 | tf_op jit(solution)/shard_map/pallas_call | solution.py:339
